TPU v7x, 256 devices: a whole 4x4x8 slice. The times are simulated.
256 devices in a mesh: pix: 8 (over y, core), pos: 32 (over z, x).
Axes of the slice: x: 4, y: 4, z: 8, core: 2. Of those that a mesh axis runs over, the one named last changes fastest.
Arguments:
- stack: bfloat16 [16384, 2, 32768], P('pix', None, 'pos'), may hold values from -6 to 6
- omega: int32 [32768, 128], P('pos'), may hold values from -32768 to 32767
Outputs:
- basis: float32 [16384, 2, 128], P('pix')
- projected: float32 [128, 32768], P('pix', 'pos')
All inputs are finite; a program needn't handle non-finite values.
Results may differ from a plain program's by a relative error of at most 0.0041.
Values may be sent and summed in bfloat16 or wider, within the bound.
A program may use at most 64 MiB of HBM per device.

v0:
```python
import math

import jax
import jax.numpy as jnp
from jax import lax
from jax.sharding import PartitionSpec as P


def contract_rows(left, right):
    return lax.dot_general(
        left, right, (((0,), (0,)), ((), ())), preferred_element_type=jnp.float32
    )


def body(stack, omega):
    pix_local = stack.shape[0]
    cols_local = stack.shape[2]
    width = omega.shape[1]
    matrix = stack.reshape(2 * pix_local, cols_local)
    test = (omega.astype(jnp.float32) / 32768.0).astype(jnp.bfloat16)
    first = lax.psum(jnp.dot(matrix, test, preferred_element_type=jnp.float32), "pos").astype(
        jnp.bfloat16
    )
    back_part = contract_rows(matrix, first)
    back = lax.psum(back_part, "pix").astype(jnp.bfloat16)
    sketch = lax.psum(jnp.dot(matrix, back, preferred_element_type=jnp.float32), "pos")
    gram_local = lax.dot_general(
        sketch,
        sketch,
        (((0,), (0,)), ((), ())),
        precision=lax.Precision.HIGHEST,
        preferred_element_type=jnp.float32,
    )
    lower = jnp.linalg.cholesky(lax.psum(gram_local, "pix"))
    inverse = lax.linalg.triangular_solve(
        lower, jnp.eye(width, dtype=lower.dtype), left_side=True, lower=True
    )
    q_full = jnp.dot(
        sketch, inverse.T, precision=lax.Precision.HIGHEST, preferred_element_type=jnp.float32
    )
    scale_factor = math.sqrt(2.0 * pix_local * lax.axis_size("pix"))
    basis = (q_full * scale_factor).reshape(pix_local, 2, width)
    q_low = q_full.astype(jnp.bfloat16)
    projected = lax.psum_scatter(
        contract_rows(q_low, matrix), "pix", scatter_dimension=0, tiled=True
    )
    return (basis, projected)


def solution(mesh):
    return jax.shard_map(
        body,
        mesh=mesh,
        in_specs=(P("pix", None, "pos"), P("pos", None)),
        out_specs=(P("pix", None, None), P("pix", "pos")),
        check_vma=False,
    )
```

profile of v0, /device:TPU:1, one launch (start us, length us, event | category | flops | bytes accessed | tf_op | source)
XLA Modules:
  0.0 523.9 jit_solution(18369654107632413538)
XLA Ops:
  7.2 0.0 copy-start.1
  7.2 0.0 all-reduce.5.cloned.1.call-start
  7.2 13.2 %reshape.19 = bf16[4096,1024]{1,0:T(8,128)(2,1)} reshape(bf16[2048,2,1024]{2,1,0:T(2,128)(2,1)} %param.2) | data formatting | bytes 16777216 | tf_op jit(solution)/shard_map/reshape | solution.py:19
  20.4 0.0 copy-done.1
  20.4 6.3 %convolution_bitcast_fusion.1 = f32[4096,128]{0,1:T(8,128)S(1)} fusion(bf16[4096,1024]{1,0:T(8,128)(2,1)} %reshape.19, s32[1024,128]{1,0:T(8,128)S(1)} %copy-done.1), kind=kOutput, calls=%fused_computation.1 | convolution fusion | flops 1074135040 | bytes 11010048 | tf_op jit(solution)/shard_map/dot_general | solution.py:21
  26.7 144.5 %all-reduce.8 = bf16[4096,128]{0,1:T(8,128)(2,1)S(1)} all-reduce(f32[4096,128]{0,1:T(8,128)S(1)} %convolution_bitcast_fusion.1), channel_id=1, replica_groups=mesh['pix'=8,'pos'=32] {'pos'}, use_global_device_ids=true, to_apply=%region_0.0 | all-reduce | flops 524288 | bytes 3145728 | tf_op jit(solution)/shard_map/psum | solution.py:21
  171.2 4.6 convolution_bitcast_fusion.2
  175.9 52.9 %all-reduce.9 = bf16[1024,128]{0,1:T(8,128)(2,1)S(1)} all-reduce(f32[1024,128]{0,1:T(8,128)S(1)} %convolution_bitcast_fusion.2), channel_id=1, replica_groups=mesh['pix'=8,'pos'=32] {'pix'}, use_global_device_ids=true, to_apply=%region_1.0 | all-reduce | flops 131072 | bytes 786432 | tf_op jit(solution)/shard_map/psum | solution.py:25
  228.8 7.6 %convolution_bitcast_fusion = f32[4096,128]{0,1:T(8,128)} fusion(bf16[4096,1024]{1,0:T(8,128)(2,1)} %reshape.19, bf16[1024,128]{0,1:T(8,128)(2,1)S(1)} %all-reduce.9), kind=kOutput, calls=%fused_computation | convolution fusion | flops 1073741824 | bytes 10747904 | tf_op jit(solution)/shard_map/dot_general | solution.py:26
  236.4 0.0 all-reduce.5.cloned.1.call-update
  236.4 0.0 all-reduce.7.cloned.1.call-start
  236.4 145.0 %all-reduce.5.cloned.1.call-done = f32[4096,128]{0,1:T(8,128)} async-done(((f32[4096,128]{0,1:T(8,128)}), f32[4096,128]{0,1:T(8,128)}) %all-reduce.5.cloned.1.call-update) | async-done | bytes 2097168 | tf_op jit(solution)/shard_map/psum | solution.py:26
  381.4 0.0 copy-start
  381.4 4.8 fusion.10
  386.3 0.0 all-reduce.7.cloned.1.call-update
  386.3 0.2 reduce-scatter.2.cloned.1.call-start
  386.5 63.2 %all-reduce.7.cloned.1.call-done = f32[128,128]{0,1:T(8,128)} async-done(((f32[128,128]{0,1:T(8,128)}), f32[128,128]{0,1:T(8,128)}) %all-reduce.7.cloned.1.call-update) | async-done | bytes 65552 | tf_op jit(solution)/shard_map/psum | solution.py:34
  449.7 0.9 copy.5
  450.7 0.9 fusion.8
  451.5 11.7 %cholesky.17 = f32[128,128]{1,0:T(8,128)S(1)} custom-call(f32[128,128]{1,0:T(8,128)S(1)} %fusion.8), custom_call_target="Cholesky" | custom-call | tf_op jit(solution)/shard_map/jit(cholesky)/cholesky | solution.py:34
  463.3 0.6 compare_reduce_fusion
  463.9 0.7 fusion.5
  464.6 9.8 %custom-call.6 = f32[1,128,128]{1,2,0:T(8,128)S(1)} custom-call(f32[1,128,128]{2,1,0:T(8,128)S(1)} %fusion.5), custom_call_target="InvertDiagBlocksLowerTriangular" | custom-call | tf_op jit(solution)/shard_map/triangular_solve | solution.py:35
  474.4 0.2 fusion.6
  474.6 0.0 copy-done
  474.6 4.8 broadcast_multiply_fusion
  479.4 5.6 %fusion = f32[128,1024]{1,0:T(8,128)} fusion(bf16[4096,1024]{1,0:T(8,128)(2,1)} %reshape.19, bf16[4096,128]{1,0:T(8,128)(2,1)S(1)} %get-tuple-element.3), kind=kOutput, calls=%fused_computation.3 | convolution fusion | flops 1073741824 | bytes 9961472 | tf_op jit(solution)/shard_map/dot_general | solution.py:10
  485.0 0.0 reduce-scatter.2.cloned.1.call-update
  485.0 32.4 %reduce-scatter.2.cloned.1.call-done = f32[16,1024]{1,0:T(8,128)} async-done(((f32[128,1024]{1,0:T(8,128)}), f32[16,1024]{1,0:T(8,128)}) %reduce-scatter.2.cloned.1.call-update) | async-done | bytes 65552 | tf_op jit(solution)/shard_map/reduce_scatter | solution.py:44
  (1 shorter events, 0.0 us)
Async XLA Ops:
  7.2 13.2 %copy-start.1 = (s32[1024,128]{1,0:T(8,128)S(1)}, s32[1024,128]{1,0:T(8,128)}, u32[]{:S(2)}) copy-start(s32[1024,128]{1,0:T(8,128)} %param.3) | copy-start | bytes 1572868
  7.2 374.3 %all-reduce.5.cloned.1.call-start = ((), (), s32[]{:S(2)}) async-start(), calls=%async_computation.1 | async-start | bytes 4194304 | tf_op jit(solution)/shard_map/psum | solution.py:26
  236.4 213.3 %all-reduce.7.cloned.1.call-start = ((), (), s32[]{:S(2)}) async-start(), calls=%async_computation.2 | async-start | bytes 131072 | tf_op jit(solution)/shard_map/psum | solution.py:34
  381.4 93.2 %copy-start = (f32[4096,128]{0,1:T(8,128)S(1)}, f32[4096,128]{0,1:T(8,128)}, u32[]{:S(2)}) copy-start(f32[4096,128]{0,1:T(8,128)} %all-reduce.5.cloned.1.call-done) | copy-start | bytes 6291460
  386.3 131.1 %reduce-scatter.2.cloned.1.call-start = ((), (), s32[]{:S(2)}) async-start(), calls=%async_computation.3 | async-start | bytes 589824 | tf_op jit(solution)/shard_map/reduce_scatter | solution.py:44
Sparse Core Ops, SparseCore 0:
  236.5 144.8 all-reduce.4
  386.4 63.2 all-reduce.6
  485.1 32.2 reduce-scatter.1
where the time goes:
time: 526 us; the launch traced here: 524 us
  waiting for transfers between devices  241 us (46%)
  blocking collectives  197 us (37%)
  matrix products  33.9 us (6%)
  other arithmetic  23.7 us (5%)
  local copies, waits for them, and re-layouts  14.1 us (3%)
  between operations  13.8 us (3%)
    psum x1, waiting for transfers between devices, body(): lax.psum(jnp.dot(matrix, back, preferred_element_type=jnp.float32), 'pos')  145 us
    psum x1, blocking collectives, body(): lax.psum(jnp.dot(matrix, test, preferred_element_type=jnp.float32), 'pos')  145 us
    psum x1, waiting for transfers between devices, body(): lower = jnp.linalg.cholesky(lax.psum(gram_local, 'pix'))  63.2 us
    psum x1, blocking collectives, body(): back = lax.psum(back_part, 'pix').astype(jnp.bfloat16)  52.9 us
    reduce_scatter x1, waiting for transfers between devices, body(): lax.psum_scatter(contract_rows(q_low, matrix), 'pix', scatter_dimension=0...  32.4 us
    reshape x1, local copies, waits for them, and re-layouts, body(): matrix = stack.reshape(2 * pix_local, cols_local)  13.2 us
    another operation x3, other arithmetic, body(): lower = jnp.linalg.cholesky(lax.psum(gram_local, 'pix'))  12.4 us
  transfers between devices with their start and end apart: 3, of which 3 were waited for; matrix products, arithmetic and copies ran while one was open for 0% of the time, Pallas kernels for 0%

commit v1 on v0

v1 whole, which is shorter than its diff:
```python
import math

import jax
import jax.numpy as jnp
from jax import lax
from jax.experimental import pallas as pl
from jax.experimental.pallas import tpu as pltpu
from jax.sharding import PartitionSpec as P

MESH = pl.DeviceIdType.MESH
K = 128
NX = 4
NZ = 8
NP = 8
ROWS = 4096
COLS = 1024
BLOCK = ROWS // NX
HALF = BLOCK // 2
CHUNK = BLOCK // NZ
FAR_FIRST = (4, 3, 5, 2, 6, 1, 7)
F32 = jnp.float32
BF16 = jnp.bfloat16


def contract(left, right, a, b):
    return lax.dot_general(left, right, (((a,), (b,)), ((), ())), preferred_element_type=F32)


class Places:
    def __init__(self):
        self.pix, self.pos = lax.axis_index("pix"), lax.axis_index("pos")
        self.z, self.x = self.pos // NX, self.pos % NX

    def at_x(self, d):
        return (self.pix, self.z * NX + (self.x + d) % NX)

    def at_z(self, d):
        return (self.pix, ((self.z + d) % NZ) * NX + self.x)

    def at_pix(self, d):
        return ((self.pix + d) % NP, self.pos)

    def block(self, d):
        return (self.x + d) % NX


def send(src, dst, sems, i, where):
    copy = pltpu.make_async_remote_copy(
        src_ref=src, dst_ref=dst, send_sem=sems.at[0, i], recv_sem=sems.at[1, i],
        device_id=where, device_id_type=MESH,
    )
    copy.start()
    return copy


def rows(start, size):
    return pl.ds(pl.multiple_of(start, size), size)


def sum_and_gather(here, compute, consume, part, held, own, relay, across, zpart, zgot, full, sems):
    copies = []
    part[0] = compute(here.block(2)).astype(BF16)
    low, high = pl.ds(0, HALF), pl.ds(HALF, HALF)
    r0 = send(part.at[0, low], relay.at[0], sems, 0, here.at_x(1))
    r1 = send(part.at[0, high], relay.at[1], sems, 1, here.at_x(3))
    one = compute(here.block(1))
    part[1, HALF:] = one[HALF:].astype(BF16)
    x0 = send(part.at[1, high], across.at[0, high], sems, 2, here.at_x(1))
    held[0] = one[:HALF]
    other = compute(here.block(3))
    part[2, :HALF] = other[:HALF].astype(BF16)
    x1 = send(part.at[2, low], across.at[1, low], sems, 3, here.at_x(3))
    held[1] = other[HALF:]
    own[...] = compute(here.block(0))
    r0.wait_recv()
    part[1, :HALF] = (held[0] + relay[0].astype(F32)).astype(BF16)
    x2 = send(part.at[1, low], across.at[0, low], sems, 4, here.at_x(1))
    r1.wait_recv()
    part[2, HALF:] = (held[1] + relay[1].astype(F32)).astype(BF16)
    x3 = send(part.at[2, high], across.at[1, high], sems, 5, here.at_x(3))
    for c in (x0, x1, x2, x3):
        c.wait_recv()
    own[...] = own[...] + across[0].astype(F32) + across[1].astype(F32)
    zpart[...] = own[...].astype(BF16)
    zs = []
    for i, d in enumerate(FAR_FIRST):
        zs.append(send(zpart.at[rows((here.z + d) % NZ * CHUNK, CHUNK)], zgot.at[i], sems, 6 + i, here.at_z(d)))
    copies += [r0, r1, x0, x1, x2, x3] + zs
    mine = own[rows(here.z * CHUNK, CHUNK), :]
    for i in range(7):
        zs[i].wait_recv()
        mine = mine + zgot[i].astype(F32)
    spot = full.at[rows((here.x * NZ + here.z) * CHUNK, CHUNK)]
    spot[...] = mine.astype(BF16)
    gs = [send(spot, spot, sems, 13 + i, here.at_z(d)) for i, d in enumerate(FAR_FIRST)]
    for c in gs:
        c.wait_recv()

    def half(d, h):
        return full.at[rows(here.block(d) * BLOCK + h * HALF, HALF)]

    a0 = send(half(0, 0), half(0, 0), sems, 20, here.at_x(1))
    b0 = send(half(0, 1), half(0, 1), sems, 21, here.at_x(3))
    b1 = send(half(0, 1), half(0, 1), sems, 22, here.at_x(1))
    a1 = send(half(0, 0), half(0, 0), sems, 23, here.at_x(3))
    consume(here.block(0))
    a0.wait_recv()
    a2 = send(half(3, 0), half(3, 0), sems, 24, here.at_x(1))
    b0.wait_recv()
    b2 = send(half(1, 1), half(1, 1), sems, 25, here.at_x(3))
    b1.wait_recv()
    consume(here.block(3))
    a1.wait_recv()
    consume(here.block(1))
    a2.wait_recv()
    b2.wait_recv()
    consume(here.block(2))
    return copies + gs + [a0, b0, b1, a1, a2, b2]


def sketch_kernel(
    stack, omega, s_out, p_out, g_out,
    m, om, test, part, held, own, relay, across, zpart, zgot, full,
    bt, bparts, bgot, back, grams, total, load_sems, sems, pix_sems,
):
    here = Places()
    barrier = pltpu.get_barrier_semaphore()
    partners = [here.at_x(1), here.at_x(3)]
    partners += [here.at_z(d) for d in FAR_FIRST] + [here.at_pix(d) for d in range(1, NP)]
    for p in partners:
        pl.semaphore_signal(barrier, inc=1, device_id=p, device_id_type=MESH)
    load_om = pltpu.make_async_copy(omega, om, load_sems.at[4])
    load_om.start()
    flat = stack.reshape(ROWS, COLS)
    loads = {}
    for i, d in enumerate((2, 1, 3, 0)):
        where = rows(here.block(d) * BLOCK, BLOCK)
        loads[i] = pltpu.make_async_copy(flat.at[where], m.at[where], load_sems.at[i])
        loads[i].start()
    load_om.wait()
    test[...] = (om[...].astype(F32) / 32768.0).astype(BF16)
    pl.semaphore_wait(barrier, len(partners))

    turn = iter(range(4))

    def first_block(b):
        loads[next(turn)].wait()
        return jnp.dot(m[rows(b * BLOCK, BLOCK), :], test[...], preferred_element_type=F32)

    def take_first(b):
        where = rows(b * BLOCK, BLOCK)
        bt[...] += contract(full[0, where, :], m[where, :], 0, 0)

    bt[...] = jnp.zeros_like(bt)
    copies = sum_and_gather(
        here, first_block, take_first, part.at[0], held.at[0], own, relay.at[0],
        across.at[0], zpart.at[0], zgot.at[0], full.at[0], sems.at[0],
    )

    for j in range(NP):
        bparts[j] = bt[:, j * K:(j + 1) * K].astype(BF16)
        total[j] = bt[:, j * K:(j + 1) * K]
    bs = []
    for d in range(1, NP):
        bs.append(send(bparts.at[(here.pix + d) % NP], bgot.at[d - 1], pix_sems.at[0], d - 1, here.at_pix(d)))
    mine = total[here.pix]
    for d in range(1, NP):
        bs[d - 1].wait_recv()
        mine = mine + bgot[d - 1].astype(F32)
    spot = back.at[rows(here.pix * K, K)]
    spot[...] = mine.T.astype(BF16)
    gs = [send(spot, spot, pix_sems.at[1], d - 1, here.at_pix(d)) for d in range(1, NP)]
    for c in gs:
        c.wait_recv()
    copies += bs + gs

    def sketch_block(b):
        return jnp.dot(m[rows(b * BLOCK, BLOCK), :], back[...], preferred_element_type=F32)

    def take_sketch(b):
        where = rows(b * BLOCK, BLOCK)
        s = full[1, where, :]
        total[b] = contract(s, s, 0, 0)
        p_out[...] += contract(s, m[where, :], 0, 0)

    p_out[...] = jnp.zeros_like(p_out)
    copies += sum_and_gather(
        here, sketch_block, take_sketch, part.at[1], held.at[1], own, relay.at[1],
        across.at[1], zpart.at[1], zgot.at[1], full.at[1], sems.at[1],
    )
    grams[here.pix] = total[0] + total[1] + total[2] + total[3]
    mine = grams.at[here.pix]
    gs = [send(mine, mine, pix_sems.at[2], d - 1, here.at_pix(d)) for d in range(1, NP)]
    s_out[...] = full[1]
    for c in gs:
        c.wait_recv()
    gram = grams[0]
    for j in range(1, NP):
        gram = gram + grams[j]
    g_out[...] = gram
    for c in copies + gs:
        c.wait_send()


def sketch_call(stack, omega):
    vmem = pl.BlockSpec(memory_space=pltpu.VMEM)
    hbm = pl.BlockSpec(memory_space=pl.ANY)
    return pl.pallas_call(
        sketch_kernel,
        out_shape=(
            jax.ShapeDtypeStruct((ROWS, K), BF16),
            jax.ShapeDtypeStruct((K, COLS), F32),
            jax.ShapeDtypeStruct((K, K), F32),
        ),
        in_specs=[hbm, hbm],
        out_specs=(vmem, vmem, vmem),
        scratch_shapes=[
            pltpu.VMEM((ROWS, COLS), BF16),
            pltpu.VMEM((COLS, K), jnp.int32),
            pltpu.VMEM((COLS, K), BF16),
            pltpu.VMEM((2, 3, BLOCK, K), BF16),
            pltpu.VMEM((2, 2, HALF, K), F32),
            pltpu.VMEM((BLOCK, K), F32),
            pltpu.VMEM((2, 2, HALF, K), BF16),
            pltpu.VMEM((2, 2, BLOCK, K), BF16),
            pltpu.VMEM((2, BLOCK, K), BF16),
            pltpu.VMEM((2, 7, CHUNK, K), BF16),
            pltpu.VMEM((2, ROWS, K), BF16),
            pltpu.VMEM((K, COLS), F32),
            pltpu.VMEM((NP, K, K), BF16),
            pltpu.VMEM((NP - 1, K, K), BF16),
            pltpu.VMEM((COLS, K), BF16),
            pltpu.VMEM((NP, K, K), F32),
            pltpu.VMEM((NP, K, K), F32),
            pltpu.SemaphoreType.DMA((5,)),
            pltpu.SemaphoreType.DMA((2, 2, 26)),
            pltpu.SemaphoreType.DMA((3, 2, NP - 1)),
        ],
        compiler_params=pltpu.CompilerParams(
            collective_id=0, has_side_effects=True, vmem_limit_bytes=48 << 20
        ),
        cost_estimate=pl.CostEstimate(flops=4 * 2 * ROWS * COLS * K, bytes_accessed=12 << 20, transcendentals=0),
    )(stack, omega)


def project_kernel(p_ref, inv_ref, o_ref, parts, got, sems):
    here = Places()
    barrier = pltpu.get_barrier_semaphore()
    for d in range(1, NP):
        pl.semaphore_signal(barrier, inc=1, device_id=here.at_pix(d), device_id_type=MESH)
    mine = lax.dot_general(
        inv_ref[...], p_ref[...], (((1,), (0,)), ((), ())),
        precision=lax.Precision.HIGHEST, preferred_element_type=F32,
    )
    parts[...] = mine.reshape(NP, K // NP, COLS)
    pl.semaphore_wait(barrier, NP - 1)
    copies = []
    for d in range(1, NP):
        copies.append(send(parts.at[(here.pix + d) % NP], got.at[d - 1], sems, d - 1, here.at_pix(d)))
    total = parts[here.pix]
    for d in range(1, NP):
        copies[d - 1].wait_recv()
        total = total + got[d - 1]
    o_ref[...] = total
    for c in copies:
        c.wait_send()


def project_call(p, inverse):
    vmem = pl.BlockSpec(memory_space=pltpu.VMEM)
    return pl.pallas_call(
        project_kernel,
        out_shape=jax.ShapeDtypeStruct((K // NP, COLS), F32),
        in_specs=[vmem, vmem],
        out_specs=vmem,
        scratch_shapes=[
            pltpu.VMEM((NP, K // NP, COLS), F32),
            pltpu.VMEM((NP - 1, K // NP, COLS), F32),
            pltpu.SemaphoreType.DMA((2, NP - 1)),
        ],
        compiler_params=pltpu.CompilerParams(
            collective_id=1, has_side_effects=True, vmem_limit_bytes=16 << 20
        ),
    )(p, inverse)


def body(stack, omega):
    sketch, p, gram = sketch_call(stack, omega)
    lower = jnp.linalg.cholesky(gram)
    inverse = lax.linalg.triangular_solve(
        lower, jnp.eye(K, dtype=F32), left_side=True, lower=True
    )
    projected = project_call(p, inverse)
    scale_factor = math.sqrt(2.0 * stack.shape[0] * lax.axis_size("pix"))
    q_full = jnp.dot(
        sketch.astype(F32), inverse.T, precision=lax.Precision.HIGHEST, preferred_element_type=F32
    )
    basis = (q_full * scale_factor).reshape(stack.shape[0], 2, K)
    return (basis, projected)


def solution(mesh):
    return jax.shard_map(
        body,
        mesh=mesh,
        in_specs=(P("pix", None, "pos"), P("pos", None)),
        out_specs=(P("pix", None, None), P("pix", "pos")),
        check_vma=False,
    )
```

time: 526 us -> 141 us (0.27)
  waiting for transfers between devices: 241 us -> 0 us
  blocking collectives: 197 us -> 0 us
  Pallas kernels: 0 us -> 113 us
  matrix products: 33.9 us -> 2.57 us
  between operations: 13.8 us -> 0.69 us
  local copies, waits for them, and re-layouts: 14.1 us -> 1.75 us
    psum x2 -> x0, waiting for transfers between devices: 208 us -> none  [the longest x1 145 us: body(): lax.psum(jnp.dot(matrix, back, preferred_element_type=jnp.float32), 'pos')]
    psum x2 -> x0, blocking collectives: 197 us -> none  [the longest x1 145 us: body(): lax.psum(jnp.dot(matrix, test, preferred_element_type=jnp.float32), 'pos')]
    pallas_call x0 -> x2, Pallas kernels: none -> 113 us  [the longest x1 103 us: sketch_call(): pl.pallas_call(sketch_kernel, out_shape=(jax.ShapeDtypeStruct((ROWS, K),...]
    reduce_scatter x1 -> x0, waiting for transfers between devices: 32.4 us -> none  [body(): lax.psum_scatter(contract_rows(q_low, matrix), 'pix', scatter_dimension=0...]
    dot_general x6 -> x1, matrix products: 33.6 us -> 2.32 us  [body(): jnp.dot(sketch.astype(F32), inverse.T, precision=lax.Precision.HIGHEST, p...]
    reshape x1 -> x0, local copies, waits for them, and re-layouts: 13.2 us -> none  [body(): matrix = stack.reshape(2 * pix_local, cols_local)]
  transfers between devices with their start and end apart: 3 -> 0, of which waited for: 3 -> 0; matrix products, arithmetic and copies ran while one was open for 0% -> 0% of each run, Pallas kernels for 0% -> 0%
where the time goes in v1:
time: 141 us
  Pallas kernels  113 us (80%)
  other arithmetic  23 us (16%)
  matrix products  2.57 us (2%)
  local copies, waits for them, and re-layouts  1.75 us (1%)
    pallas_call x1, Pallas kernels, sketch_call(): pl.pallas_call(sketch_kernel, out_shape=(jax.ShapeDtypeStruct((ROWS, K),...  103 us
    another operation x3, other arithmetic, body(): lower = jnp.linalg.cholesky(gram)  12.6 us
    another operation x2, other arithmetic, body(): lax.linalg.triangular_solve(lower, jnp.eye(K, dtype=F32), left_side=True,...  10.5 us
    pallas_call x1, Pallas kernels, project_call(): pl.pallas_call(project_kernel, out_shape=jax.ShapeDtypeStruct((K // NP, C...  9.9 us

profile of v1, /device:TPU:1, one launch (start us, length us, event | category | flops | bytes accessed | tf_op | source)
XLA Modules:
  0.0 140.9 jit_solution(7323529343274328508)
XLA Ops:
  0.6 0.0 copy-start
  0.6 1.0 copy-done
  1.7 103.0 %shard_map.41 = (bf16[4096,128]{1,0:T(8,128)(2,1)S(1)}, f32[128,1024]{1,0:T(8,128)S(1)}, f32[128,128]{1,0:T(8,128)S(1)}) custom-call(bf16[2048,2,1024]{2,1,0:T(2,128)(2,1)} %stack.1, s32[1024,128]{1,0:T(8,128)S(1)} %copy-done), custom_call_target="tpu_custom_call" | custom-call | flops 4294967296 | bytes 12582912 | tf_op jit(solution)/shard_map/pallas_call | solution.py:208
  104.7 0.1 copy.4
  104.8 11.9 %cholesky.17 = f32[128,128]{1,0:T(8,128)S(1)} custom-call(f32[128,128]{1,0:T(8,128)S(1)} %fusion.3), custom_call_target="Cholesky" | custom-call | tf_op jit(solution)/shard_map/jit(cholesky)/cholesky | solution.py:289
  116.7 0.6 compare_reduce_fusion
  117.3 0.7 fusion
  118.0 9.8 %custom-call.6 = f32[1,128,128]{1,2,0:T(8,128)S(1)} custom-call(f32[1,128,128]{2,1,0:T(8,128)S(1)} %fusion), custom_call_target="InvertDiagBlocksLowerTriangular" | custom-call | tf_op jit(solution)/shard_map/triangular_solve | solution.py:290
  127.8 0.2 fusion.1.inv_ref
  128.1 9.9 %shard_map.42 = f32[16,1024]{1,0:T(8,128)S(1)} custom-call(f32[128,1024]{1,0:T(8,128)S(1)} %get-tuple-element.7.p_ref, f32[128,128]{1,0:T(8,128)S(1)} %fusion.1.inv_ref), custom_call_target="tpu_custom_call" | custom-call | tf_op jit(solution)/shard_map/pallas_call | solution.py:271
  138.0 2.3 %convolution_multiply_fusion = f32[4096,128]{1,0:T(8,128)} fusion(bf16[4096,128]{1,0:T(8,128)(2,1)S(1)} %get-tuple-element.5, f32[128,128]{1,0:T(8,128)S(1)} %fusion.1.inv_ref), kind=kOutput, calls=%fused_computation | convolution fusion | flops 805830656 | bytes 3211264 | tf_op jit(solution)/shard_map/dot_general | solution.py:295
  140.3 0.6 copy.6
  (2 shorter events, 0.0 us)
Async XLA Ops:
  0.6 1.0 copy-start

commit v2 on v1

v2 whole, which is shorter than its diff:
```python
import math

import jax
import jax.numpy as jnp
from jax import lax
from jax.experimental import pallas as pl
from jax.experimental.pallas import tpu as pltpu
from jax.sharding import PartitionSpec as P

MESH = pl.DeviceIdType.MESH
K = 128
NX = 4
NZ = 8
NP = 8
ROWS = 4096
COLS = 1024
BLOCK = ROWS // NX
CHUNK = BLOCK // NZ
FAR_FIRST = (4, 3, 5, 2, 6, 1, 7, 0)
NEAR_FIRST = (0, 1, 7, 2, 6, 3, 5, 4)
LAG = 2
PANEL = 32
HALF_K = K // 2
SCALE = math.sqrt(float(ROWS * NP))
F32 = jnp.float32
BF16 = jnp.bfloat16


def contract(left, right, a, b):
    return lax.dot_general(left, right, (((a,), (b,)), ((), ())), preferred_element_type=F32)


class Places:
    def __init__(self):
        self.pix, self.pos = lax.axis_index("pix"), lax.axis_index("pos")
        self.z, self.x = self.pos // NX, self.pos % NX

    def at_x(self, d):
        return (self.pix, self.z * NX + (self.x + d) % NX)

    def at_z(self, d):
        return (self.pix, ((self.z + d) % NZ) * NX + self.x)

    def at_pix(self, d):
        return ((self.pix + d) % NP, self.pos)

    def block(self, d):
        return (self.x + d) % NX


def send(src, dst, sems, i, where):
    copy = pltpu.make_async_remote_copy(
        src_ref=src, dst_ref=dst, send_sem=sems.at[0, i], recv_sem=sems.at[1, i],
        device_id=where, device_id_type=MESH,
    )
    copy.start()
    return copy


def rows(start, size):
    return pl.ds(pl.multiple_of(start, size), size)


def sum_and_gather(here, compute, consume, part, held, own, relay, across, zpart, zgot, full, sems):
    done = []

    def chunk(i):
        return rows((here.z + FAR_FIRST[i]) % NZ * CHUNK, CHUNK)

    part[0] = compute(here.block(2)).astype(BF16)
    relays = []
    for i in range(NZ):
        relays.append(send(part.at[0, chunk(i)], relay.at[i], sems, i, here.at_x(1 if i % 2 == 0 else 3)))
    plus, minus = {}, {}
    held[0] = compute(here.block(1))
    part[1] = held[0].astype(BF16)
    for i in range(1, NZ, 2):
        plus[i] = send(part.at[1, chunk(i)], across.at[0, i], sems, NZ + i, here.at_x(1))
    held[1] = compute(here.block(3))
    part[2] = held[1].astype(BF16)
    for i in range(0, NZ, 2):
        minus[i] = send(part.at[2, chunk(i)], across.at[1, i], sems, 2 * NZ + i, here.at_x(3))
    own[...] = compute(here.block(0))
    zs = []
    mine = None
    for step in range(NZ + LAG):
        if step < NZ:
            i = step
            relays[i].wait_recv()
            if i % 2 == 0:
                part[1, chunk(i)] = (held[0, chunk(i)] + relay[i].astype(F32)).astype(BF16)
                plus[i] = send(part.at[1, chunk(i)], across.at[0, i], sems, NZ + i, here.at_x(1))
            else:
                part[2, chunk(i)] = (held[1, chunk(i)] + relay[i].astype(F32)).astype(BF16)
                minus[i] = send(part.at[2, chunk(i)], across.at[1, i], sems, 2 * NZ + i, here.at_x(3))
        if step >= LAG:
            i = step - LAG
            plus[i].wait_recv()
            minus[i].wait_recv()
            mine = own[chunk(i), :] + across[0, i].astype(F32) + across[1, i].astype(F32)
            if i < NZ - 1:
                zpart[i] = mine.astype(BF16)
                zs.append(send(zpart.at[i], zgot.at[i], sems, 3 * NZ + i, here.at_z(FAR_FIRST[i])))
    for i in range(NZ - 1):
        zs[i].wait_recv()
        mine = mine + zgot[i].astype(F32)
    done += relays + list(plus.values()) + list(minus.values()) + zs

    def place(dx, dz):
        return full.at[rows((here.block(dx) * NZ + (here.z + dz) % NZ) * CHUNK, CHUNK)]

    spot = place(0, 0)
    spot[...] = mine.astype(BF16)
    gs = {}
    for d in NEAR_FIRST[1:]:
        gs[d] = send(spot, spot, sems, 4 * NZ + d, here.at_z(d))
    plus, minus, forward = [], [], []
    for step in range(NZ + LAG):
        if step < NZ:
            d = NEAR_FIRST[step]
            if d:
                gs[NZ - d].wait_recv()
            spot = place(0, d)
            plus.append(send(spot, spot, sems, 5 * NZ + step, here.at_x(1)))
            minus.append(send(spot, spot, sems, 6 * NZ + step, here.at_x(3)))
        if step == NZ - 1:
            consume(here.block(0))
        if step >= LAG:
            i = step - LAG
            d = NEAR_FIRST[i]
            if i % 2 == 0:
                plus[i].wait_recv()
                spot, to = place(3, d), here.at_x(1)
            else:
                minus[i].wait_recv()
                spot, to = place(1, d), here.at_x(3)
            forward.append(send(spot, spot, sems, 7 * NZ + i, to))
    for i in range(1, NZ, 2):
        plus[i].wait_recv()
    consume(here.block(3))
    for i in range(0, NZ, 2):
        minus[i].wait_recv()
    consume(here.block(1))
    for i in range(NZ):
        forward[i].wait_recv()
    consume(here.block(2))
    return done + list(gs.values()) + plus + minus + forward


def inverse_factor(gram):
    ids = lax.broadcasted_iota(jnp.int32, (K, K), 0)
    a, v = gram, (ids == lax.broadcasted_iota(jnp.int32, (K, K), 1)).astype(F32)
    row = lax.broadcasted_iota(jnp.int32, (PANEL, K), 0)
    out = []
    for lo in range(0, K, PANEL):
        ap, vp = a[:PANEL], v[:PANEL]
        c = jnp.stack([jnp.broadcast_to(ap[:, lo + k:lo + k + 1], (PANEL, K)) for k in range(PANEL)])
        for j in range(PANEL):
            r = lax.rsqrt(jnp.broadcast_to(c[0, j:j + 1], (PANEL, K)))
            below = jnp.where(row > j, c[0] * r, 0.0)
            ra, rv = ap[j:j + 1] * r, vp[j:j + 1] * r
            ap = jnp.where(row == j, ra, ap - below * ra)
            vp = jnp.where(row == j, rv, vp - below * rv)
            if j + 1 < PANEL:
                c = c[1:]
                c = c - below[None] * (c[:, j:j + 1, :] * r[None])
        out.append(vp)
        if lo + PANEL < K:
            both = lax.dot_general(
                ap, jnp.concatenate([ap, vp], axis=1), (((0,), (0,)), ((), ())),
                precision=lax.Precision.HIGHEST, preferred_element_type=F32,
            )
            a = a[PANEL:] - both[lo + PANEL:, :K]
            v = v[PANEL:] - both[lo + PANEL:, K:]
    return jnp.concatenate(out, axis=0)


def whole_kernel(
    stack, omega, basis_out, projected_out,
    m, om, test, part, held, own, relay, across, zpart, zgot, full,
    bt, bparts, bgot, back, total, mine_gram, half_got, halves, gram, pparts, pgot,
    load_sems, sems, pix_sems, gram_sems,
):
    here = Places()
    barrier = pltpu.get_barrier_semaphore()
    partners = [here.at_x(1), here.at_x(3)]
    partners += [here.at_z(d) for d in range(1, NZ)] + [here.at_pix(d) for d in range(1, NP)]
    for p in partners:
        pl.semaphore_signal(barrier, inc=1, device_id=p, device_id_type=MESH)
    load_om = pltpu.make_async_copy(omega, om, load_sems.at[4])
    load_om.start()
    flat = stack.reshape(ROWS, COLS)
    loads = []
    for i, d in enumerate((2, 1, 3, 0)):
        where = rows(here.block(d) * BLOCK, BLOCK)
        loads.append(pltpu.make_async_copy(flat.at[where], m.at[where], load_sems.at[i]))
        loads[i].start()
    load_om.wait()
    test[...] = (om[...].astype(F32) / 32768.0).astype(BF16)
    pl.semaphore_wait(barrier, len(partners))

    turn = iter(loads)

    def first_block(b):
        next(turn).wait()
        return jnp.dot(m[rows(b * BLOCK, BLOCK), :], test[...], preferred_element_type=F32)

    def take_first(b):
        where = rows(b * BLOCK, BLOCK)
        bt[...] += contract(full[0, where, :], m[where, :], 0, 0)

    bt[...] = jnp.zeros_like(bt)
    copies = sum_and_gather(
        here, first_block, take_first, part.at[0], held, own, relay.at[0],
        across.at[0], zpart.at[0], zgot.at[0], full.at[0], sems.at[0],
    )

    for j in range(NP):
        bparts[j] = bt[:, j * K:(j + 1) * K].astype(BF16)
        total[j] = bt[:, j * K:(j + 1) * K]
    bs = []
    for d in range(1, NP):
        bs.append(send(bparts.at[(here.pix + d) % NP], bgot.at[d - 1], pix_sems.at[0], d - 1, here.at_pix(d)))
    mine = total[here.pix]
    for d in range(1, NP):
        bs[d - 1].wait_recv()
        mine = mine + bgot[d - 1].astype(F32)
    spot = back.at[rows(here.pix * K, K)]
    spot[...] = mine.T.astype(BF16)
    gs = [send(spot, spot, pix_sems.at[1], d - 1, here.at_pix(d)) for d in range(1, NP)]
    for c in gs:
        c.wait_recv()
    copies += bs + gs

    def sketch_block(b):
        return jnp.dot(m[rows(b * BLOCK, BLOCK), :], back[...], preferred_element_type=F32)

    def take_sketch(b):
        where = rows(b * BLOCK, BLOCK)
        s = full[1, where, :]
        total[b] = contract(s, s, 0, 0)
        bt[...] += contract(s, m[where, :], 0, 0)

    bt[...] = jnp.zeros_like(bt)
    copies += sum_and_gather(
        here, sketch_block, take_sketch, part.at[1], held, own, relay.at[1],
        across.at[1], zpart.at[1], zgot.at[1], full.at[1], sems.at[1],
    )

    y, core = here.pix // 2, here.pix % 2
    near = (y * 2 + 1 - core, here.pos)
    mine_gram[...] = total[0] + total[1] + total[2] + total[3]
    keep, give = rows(core * HALF_K, HALF_K), rows((1 - core) * HALF_K, HALF_K)
    swap = send(mine_gram.at[give], half_got, gram_sems, 0, near)
    swap.wait_recv()
    halves[y] = mine_gram[keep, :] + half_got[...]
    spot = halves.at[y]
    ys = [send(spot, spot, gram_sems, d, ((y + d) % 4 * 2 + core, here.pos)) for d in (1, 2, 3)]
    for c in ys:
        c.wait_recv()
    gram[keep, :] = (halves[0] + halves[1]) + (halves[2] + halves[3])
    spot = gram.at[keep]
    swap_back = send(spot, spot, gram_sems, 4, near)
    swap_back.wait_recv()
    copies += [swap, swap_back] + ys
    inverse = inverse_factor(gram[...])

    product = lax.dot_general(
        inverse, bt[...], (((1,), (0,)), ((), ())),
        precision=lax.Precision.HIGHEST, preferred_element_type=F32,
    )
    bt[...] = product
    pparts[...] = product.astype(BF16)
    share = K // NP
    ps = []
    for d in range(1, NP):
        to = (here.pix + d) % NP
        ps.append(send(pparts.at[rows(to * share, share)], pgot.at[d - 1], pix_sems.at[2], d - 1, here.at_pix(d)))

    scaled = inverse.T * SCALE
    top = scaled.astype(BF16)
    rest = scaled - top.astype(F32)
    mid = rest.astype(BF16)
    low = (rest - mid.astype(F32)).astype(BF16)
    for b in range(NX):
        where = pl.ds(b * BLOCK, BLOCK)
        s = full[1, where, :]
        basis_out[where, :] = (
            jnp.dot(s, top, preferred_element_type=F32)
            + jnp.dot(s, mid, preferred_element_type=F32)
            + jnp.dot(s, low, preferred_element_type=F32)
        )
    mine = bt[rows(here.pix * share, share), :]
    for d in range(1, NP):
        ps[d - 1].wait_recv()
        mine = mine + pgot[d - 1].astype(F32)
    projected_out[...] = mine
    for c in copies + ps:
        c.wait_send()


def body(stack, omega):
    vmem = pl.BlockSpec(memory_space=pltpu.VMEM)
    hbm = pl.BlockSpec(memory_space=pl.ANY)
    basis, projected = pl.pallas_call(
        whole_kernel,
        out_shape=(
            jax.ShapeDtypeStruct((ROWS, K), F32),
            jax.ShapeDtypeStruct((K // NP, COLS), F32),
        ),
        in_specs=[hbm, hbm],
        out_specs=(vmem, vmem),
        scratch_shapes=[
            pltpu.VMEM((ROWS, COLS), BF16),
            pltpu.VMEM((COLS, K), jnp.int32),
            pltpu.VMEM((COLS, K), BF16),
            pltpu.VMEM((2, 3, BLOCK, K), BF16),
            pltpu.VMEM((2, BLOCK, K), F32),
            pltpu.VMEM((BLOCK, K), F32),
            pltpu.VMEM((2, NZ, CHUNK, K), BF16),
            pltpu.VMEM((2, 2, NZ, CHUNK, K), BF16),
            pltpu.VMEM((2, NZ - 1, CHUNK, K), BF16),
            pltpu.VMEM((2, NZ - 1, CHUNK, K), BF16),
            pltpu.VMEM((2, ROWS, K), BF16),
            pltpu.VMEM((K, COLS), F32),
            pltpu.VMEM((NP, K, K), BF16),
            pltpu.VMEM((NP - 1, K, K), BF16),
            pltpu.VMEM((COLS, K), BF16),
            pltpu.VMEM((NP, K, K), F32),
            pltpu.VMEM((K, K), F32),
            pltpu.VMEM((HALF_K, K), F32),
            pltpu.VMEM((4, HALF_K, K), F32),
            pltpu.VMEM((K, K), F32),
            pltpu.VMEM((K, COLS), BF16),
            pltpu.VMEM((NP - 1, K // NP, COLS), BF16),
            pltpu.SemaphoreType.DMA((5,)),
            pltpu.SemaphoreType.DMA((2, 2, 8 * NZ)),
            pltpu.SemaphoreType.DMA((3, 2, NP - 1)),
            pltpu.SemaphoreType.DMA((2, 5)),
        ],
        compiler_params=pltpu.CompilerParams(
            collective_id=0, has_side_effects=True, vmem_limit_bytes=48 << 20
        ),
        cost_estimate=pl.CostEstimate(flops=4 * 2 * ROWS * COLS * K, bytes_accessed=12 << 20, transcendentals=0),
    )(stack, omega)
    return basis.reshape(stack.shape[0], 2, K), projected


def solution(mesh):
    return jax.shard_map(
        body,
        mesh=mesh,
        in_specs=(P("pix", None, "pos"), P("pos", None)),
        out_specs=(P("pix", None, None), P("pix", "pos")),
        check_vma=False,
    )
```

time: 141 us -> 116 us (0.82)
  other arithmetic: 23 us -> 0 us
  matrix products: 2.57 us -> 0 us
    another operation x5 -> x0, other arithmetic: 23 us -> none  [the longest x3 12.6 us: body(): lower = jnp.linalg.cholesky(gram)]
    dot_general x1 -> x0, matrix products: 2.32 us -> none  [body(): jnp.dot(sketch.astype(F32), inverse.T, precision=lax.Precision.HIGHEST, p...]
    unnamed x3 -> x4, local copies, waits for them, and re-layouts: 1.66 us -> 2.99 us
    pallas_call x2 -> x1, Pallas kernels: 113 us -> 112 us  [body(): pl.pallas_call(whole_kernel, out_shape=(jax.ShapeDtypeStruct((ROWS, K), F...]
where the time goes in v2:
time: 116 us; the launch traced here: 115 us
  Pallas kernels  112 us (97%)
  local copies, waits for them, and re-layouts  2.99 us (3%)
    pallas_call x1, Pallas kernels, body(): pl.pallas_call(whole_kernel, out_shape=(jax.ShapeDtypeStruct((ROWS, K), F...  112 us
    unnamed x4, local copies, waits for them, and re-layouts  2.99 us

profile of v2, /device:TPU:1, one launch (start us, length us, event | category | flops | bytes accessed | tf_op | source)
XLA Modules:
  0.0 115.4 jit_solution(6108952479550155501)
XLA Ops:
  0.6 0.0 copy-start
  0.6 1.0 copy-done
  1.7 111.8 %shard_map.41 = (f32[4096,128]{1,0:T(8,128)S(1)}, f32[16,1024]{1,0:T(8,128)S(1)}) custom-call(bf16[2048,2,1024]{2,1,0:T(2,128)(2,1)} %stack.1, s32[1024,128]{1,0:T(8,128)S(1)} %copy-done), custom_call_target="tpu_custom_call" | custom-call | flops 4294967296 | bytes 12582912 | tf_op jit(solution)/shard_map/pallas_call | solution.py:305
  113.5 1.3 %copy.6 = f32[2048,2,128]{2,1,0:T(2,128)} copy(f32[2048,2,128]{2,1,0:T(2,128)S(1)} %bitcast.1) | data formatting | bytes 4194304
  114.8 0.6 copy.7
Async XLA Ops:
  0.6 1.0 copy-start

commit v3 on v2

--- a/solution.py
+++ b/solution.py
@@ -19,6 +19,8 @@
 FAR_FIRST = (4, 3, 5, 2, 6, 1, 7, 0)
 NEAR_FIRST = (0, 1, 7, 2, 6, 3, 5, 4)
 LAG = 2
+RELAYED = (4, 5, 6, 7)
+FORWARDED = (0, 1)
 PANEL = 32
 HALF_K = K // 2
 SCALE = math.sqrt(float(ROWS * NP))
@@ -61,36 +63,43 @@
     return pl.ds(pl.multiple_of(start, size), size)
 
 
-def sum_and_gather(here, compute, consume, part, held, own, relay, across, zpart, zgot, full, sems):
+def sum_and_gather(here, compute, consume, part, held, own, relay, across, zpart, zgot, full, sems, enter=None):
     done = []
 
     def chunk(i):
         return rows((here.z + FAR_FIRST[i]) % NZ * CHUNK, CHUNK)
 
     part[0] = compute(here.block(2)).astype(BF16)
+    if enter is not None:
+        enter()
     relays = []
     for i in range(NZ):
-        relays.append(send(part.at[0, chunk(i)], relay.at[i], sems, i, here.at_x(1 if i % 2 == 0 else 3)))
-    plus, minus = {}, {}
+        if i in RELAYED:
+            relays.append(send(part.at[0, chunk(i)], relay.at[i], sems, i, here.at_x(1 if i % 2 == 0 else 3)))
+        else:
+            relays.append(send(part.at[0, chunk(i)], across.at[2, i], sems, i, here.at_x(2)))
     held[0] = compute(here.block(1))
     part[1] = held[0].astype(BF16)
-    for i in range(1, NZ, 2):
-        plus[i] = send(part.at[1, chunk(i)], across.at[0, i], sems, NZ + i, here.at_x(1))
     held[1] = compute(here.block(3))
     part[2] = held[1].astype(BF16)
-    for i in range(0, NZ, 2):
-        minus[i] = send(part.at[2, chunk(i)], across.at[1, i], sems, 2 * NZ + i, here.at_x(3))
     own[...] = compute(here.block(0))
+    plus, minus = {}, {}
+    for i in range(NZ):
+        if i % 2 == 1 or i not in RELAYED:
+            plus[i] = send(part.at[1, chunk(i)], across.at[0, i], sems, NZ + i, here.at_x(1))
+        if i % 2 == 0 or i not in RELAYED:
+            minus[i] = send(part.at[2, chunk(i)], across.at[1, i], sems, 2 * NZ + i, here.at_x(3))
     zs = []
     mine = None
     for step in range(NZ + LAG):
         if step < NZ:
             i = step
-            relays[i].wait_recv()
-            if i % 2 == 0:
+            if i in RELAYED:
+                relays[i].wait_recv()
+            if i in RELAYED and i % 2 == 0:
                 part[1, chunk(i)] = (held[0, chunk(i)] + relay[i].astype(F32)).astype(BF16)
                 plus[i] = send(part.at[1, chunk(i)], across.at[0, i], sems, NZ + i, here.at_x(1))
-            else:
+            elif i in RELAYED:
                 part[2, chunk(i)] = (held[1, chunk(i)] + relay[i].astype(F32)).astype(BF16)
                 minus[i] = send(part.at[2, chunk(i)], across.at[1, i], sems, 2 * NZ + i, here.at_x(3))
         if step >= LAG:
@@ -98,6 +107,9 @@
             plus[i].wait_recv()
             minus[i].wait_recv()
             mine = own[chunk(i), :] + across[0, i].astype(F32) + across[1, i].astype(F32)
+            if i not in RELAYED:
+                relays[i].wait_recv()
+                mine = mine + across[2, i].astype(F32)
             if i < NZ - 1:
                 zpart[i] = mine.astype(BF16)
                 zs.append(send(zpart.at[i], zgot.at[i], sems, 3 * NZ + i, here.at_z(FAR_FIRST[i])))
@@ -114,7 +126,7 @@
     gs = {}
     for d in NEAR_FIRST[1:]:
         gs[d] = send(spot, spot, sems, 4 * NZ + d, here.at_z(d))
-    plus, minus, forward = [], [], []
+    plus, minus, forward = [], [], {}
     for step in range(NZ + LAG):
         if step < NZ:
             d = NEAR_FIRST[step]
@@ -123,28 +135,34 @@
             spot = place(0, d)
             plus.append(send(spot, spot, sems, 5 * NZ + step, here.at_x(1)))
             minus.append(send(spot, spot, sems, 6 * NZ + step, here.at_x(3)))
+            if step not in FORWARDED:
+                forward[step] = send(spot, spot, sems, 7 * NZ + step, here.at_x(2))
         if step == NZ - 1:
             consume(here.block(0))
         if step >= LAG:
             i = step - LAG
             d = NEAR_FIRST[i]
+            if i not in FORWARDED:
+                continue
             if i % 2 == 0:
                 plus[i].wait_recv()
                 spot, to = place(3, d), here.at_x(1)
             else:
                 minus[i].wait_recv()
                 spot, to = place(1, d), here.at_x(3)
-            forward.append(send(spot, spot, sems, 7 * NZ + i, to))
-    for i in range(1, NZ, 2):
-        plus[i].wait_recv()
+            forward[i] = send(spot, spot, sems, 7 * NZ + i, to)
+    for i in range(NZ):
+        if i % 2 == 1 or i not in FORWARDED:
+            plus[i].wait_recv()
     consume(here.block(3))
-    for i in range(0, NZ, 2):
-        minus[i].wait_recv()
+    for i in range(NZ):
+        if i % 2 == 0 or i not in FORWARDED:
+            minus[i].wait_recv()
     consume(here.block(1))
     for i in range(NZ):
         forward[i].wait_recv()
     consume(here.block(2))
-    return done + list(gs.values()) + plus + minus + forward
+    return done + list(gs.values()) + plus + minus + list(forward.values())
 
 
 def inverse_factor(gram):
@@ -175,15 +193,22 @@
     return jnp.concatenate(out, axis=0)
 
 
+def thirds(value):
+    top = value.astype(BF16)
+    rest = value - top.astype(F32)
+    mid = rest.astype(BF16)
+    return top, mid, (rest - mid.astype(F32)).astype(BF16)
+
+
 def whole_kernel(
     stack, omega, basis_out, projected_out,
     m, om, test, part, held, own, relay, across, zpart, zgot, full,
-    bt, bparts, bgot, back, total, mine_gram, half_got, halves, gram, pparts, pgot,
+    bt, bparts, bgot, back, total, mine_gram, half_got, halves, gram, factor, pparts, pgot, pall,
     load_sems, sems, pix_sems, gram_sems,
 ):
     here = Places()
     barrier = pltpu.get_barrier_semaphore()
-    partners = [here.at_x(1), here.at_x(3)]
+    partners = [here.at_x(d) for d in range(1, NX)]
     partners += [here.at_z(d) for d in range(1, NZ)] + [here.at_pix(d) for d in range(1, NP)]
     for p in partners:
         pl.semaphore_signal(barrier, inc=1, device_id=p, device_id_type=MESH)
@@ -197,8 +222,6 @@
         loads[i].start()
     load_om.wait()
     test[...] = (om[...].astype(F32) / 32768.0).astype(BF16)
-    pl.semaphore_wait(barrier, len(partners))
-
     turn = iter(loads)
 
     def first_block(b):
@@ -213,6 +236,7 @@
     copies = sum_and_gather(
         here, first_block, take_first, part.at[0], held, own, relay.at[0],
         across.at[0], zpart.at[0], zgot.at[0], full.at[0], sems.at[0],
+        lambda: pl.semaphore_wait(barrier, len(partners)),
     )
 
     for j in range(NP):
@@ -256,32 +280,31 @@
     halves[y] = mine_gram[keep, :] + half_got[...]
     spot = halves.at[y]
     ys = [send(spot, spot, gram_sems, d, ((y + d) % 4 * 2 + core, here.pos)) for d in (1, 2, 3)]
+    for j in range(NP):
+        pparts[j] = bt[:, j * K:(j + 1) * K].astype(BF16)
+        total[j] = bt[:, j * K:(j + 1) * K]
+    ps = []
+    for d in range(1, NP):
+        ps.append(send(pparts.at[(here.pix + d) % NP], pgot.at[d - 1], pix_sems.at[2], d - 1, here.at_pix(d)))
     for c in ys:
         c.wait_recv()
     gram[keep, :] = (halves[0] + halves[1]) + (halves[2] + halves[3])
     spot = gram.at[keep]
     swap_back = send(spot, spot, gram_sems, 4, near)
+    mine = total[here.pix]
+    for d in range(1, NP):
+        ps[d - 1].wait_recv()
+        mine = mine + pgot[d - 1].astype(F32)
+    pall[here.pix] = mine.astype(BF16)
+    spot = pall.at[here.pix]
+    gs = [send(spot, spot, pix_sems.at[3], d - 1, here.at_pix(d)) for d in range(1, NP)]
     swap_back.wait_recv()
-    copies += [swap, swap_back] + ys
+    copies += [swap, swap_back] + ys + ps + gs
     inverse = inverse_factor(gram[...])
-
-    product = lax.dot_general(
-        inverse, bt[...], (((1,), (0,)), ((), ())),
-        precision=lax.Precision.HIGHEST, preferred_element_type=F32,
-    )
-    bt[...] = product
-    pparts[...] = product.astype(BF16)
-    share = K // NP
-    ps = []
-    for d in range(1, NP):
-        to = (here.pix + d) % NP
-        ps.append(send(pparts.at[rows(to * share, share)], pgot.at[d - 1], pix_sems.at[2], d - 1, here.at_pix(d)))
+    factor[...] = inverse
 
     scaled = inverse.T * SCALE
-    top = scaled.astype(BF16)
-    rest = scaled - top.astype(F32)
-    mid = rest.astype(BF16)
-    low = (rest - mid.astype(F32)).astype(BF16)
+    top, mid, low = thirds(scaled)
     for b in range(NX):
         where = pl.ds(b * BLOCK, BLOCK)
         s = full[1, where, :]
@@ -290,12 +313,14 @@
             + jnp.dot(s, mid, preferred_element_type=F32)
             + jnp.dot(s, low, preferred_element_type=F32)
         )
-    mine = bt[rows(here.pix * share, share), :]
-    for d in range(1, NP):
-        ps[d - 1].wait_recv()
-        mine = mine + pgot[d - 1].astype(F32)
-    projected_out[...] = mine
-    for c in copies + ps:
+    share = K // NP
+    lines = jnp.concatenate(thirds(factor[rows(here.pix * share, share), :]), axis=0)
+    for c in gs:
+        c.wait_recv()
+    for j in range(NP):
+        product = jnp.dot(lines, pall[j], preferred_element_type=F32)
+        projected_out[:, j * K:(j + 1) * K] = product[:share] + product[share:2 * share] + product[2 * share:]
+    for c in copies:
         c.wait_send()
 
 
@@ -308,7 +333,7 @@
             jax.ShapeDtypeStruct((ROWS, K), F32),
             jax.ShapeDtypeStruct((K // NP, COLS), F32),
         ),
-        in_specs=[hbm, hbm],
+        in_specs=[hbm, pl.BlockSpec(memory_space=pltpu.HBM)],
         out_specs=(vmem, vmem),
         scratch_shapes=[
             pltpu.VMEM((ROWS, COLS), BF16),
@@ -318,7 +343,7 @@
             pltpu.VMEM((2, BLOCK, K), F32),
             pltpu.VMEM((BLOCK, K), F32),
             pltpu.VMEM((2, NZ, CHUNK, K), BF16),
-            pltpu.VMEM((2, 2, NZ, CHUNK, K), BF16),
+            pltpu.VMEM((2, 3, NZ, CHUNK, K), BF16),
             pltpu.VMEM((2, NZ - 1, CHUNK, K), BF16),
             pltpu.VMEM((2, NZ - 1, CHUNK, K), BF16),
             pltpu.VMEM((2, ROWS, K), BF16),
@@ -331,11 +356,13 @@
             pltpu.VMEM((HALF_K, K), F32),
             pltpu.VMEM((4, HALF_K, K), F32),
             pltpu.VMEM((K, K), F32),
-            pltpu.VMEM((K, COLS), BF16),
-            pltpu.VMEM((NP - 1, K // NP, COLS), BF16),
+            pltpu.VMEM((K, K), F32),
+            pltpu.VMEM((NP, K, K), BF16),
+            pltpu.VMEM((NP - 1, K, K), BF16),
+            pltpu.VMEM((NP, K, K), BF16),
             pltpu.SemaphoreType.DMA((5,)),
             pltpu.SemaphoreType.DMA((2, 2, 8 * NZ)),
-            pltpu.SemaphoreType.DMA((3, 2, NP - 1)),
+            pltpu.SemaphoreType.DMA((4, 2, NP - 1)),
             pltpu.SemaphoreType.DMA((2, 5)),
         ],
         compiler_params=pltpu.CompilerParams(

time: 116 us -> 105 us (0.905)
  Pallas kernels: 112 us -> 102 us
    pallas_call x1, Pallas kernels: 112 us -> 102 us  [body(): pl.pallas_call(whole_kernel, out_shape=(jax.ShapeDtypeStruct((ROWS, K), F...]
where the time goes in v3:
time: 105 us
  Pallas kernels  102 us (97%)
  local copies, waits for them, and re-layouts  2.99 us (3%)
    pallas_call x1, Pallas kernels, body(): pl.pallas_call(whole_kernel, out_shape=(jax.ShapeDtypeStruct((ROWS, K), F...  102 us
    unnamed x4, local copies, waits for them, and re-layouts  2.99 us

profile of v3, /device:TPU:1, one launch (start us, length us, event | category | flops | bytes accessed | tf_op | source)
XLA Modules:
  0.0 105.2 jit_solution(17598793155460450139)
XLA Ops:
  0.6 0.0 copy-start
  0.6 1.0 copy-done
  1.7 101.6 %shard_map.41 = (f32[4096,128]{1,0:T(8,128)S(1)}, f32[16,1024]{1,0:T(8,128)S(1)}) custom-call(bf16[2048,2,1024]{2,1,0:T(2,128)(2,1)} %stack.1, s32[1024,128]{1,0:T(8,128)S(1)} %copy-done), custom_call_target="tpu_custom_call" | custom-call | flops 4294967296 | bytes 12582912 | tf_op jit(solution)/shard_map/pallas_call | solution.py:330
  103.3 1.3 %copy.6 = f32[2048,2,128]{2,1,0:T(2,128)} copy(f32[2048,2,128]{2,1,0:T(2,128)S(1)} %bitcast.1) | data formatting | bytes 4194304
  104.6 0.6 copy.7
Async XLA Ops:
  0.6 1.0 copy-start

commit v4 on v3

--- a/solution.py
+++ b/solution.py
@@ -16,11 +16,12 @@
 COLS = 1024
 BLOCK = ROWS // NX
 CHUNK = BLOCK // NZ
-FAR_FIRST = (4, 3, 5, 2, 6, 1, 7, 0)
-NEAR_FIRST = (0, 1, 7, 2, 6, 3, 5, 4)
+FAR = (4, 3, 5, 2, 6)
+RELAYED = (3, 4)
+BACK = (2, 6, 3, 5, 4)
 LAG = 2
-RELAYED = (4, 5, 6, 7)
-FORWARDED = (0, 1)
+HOME = 1
+SIDE = 1
 PANEL = 32
 HALF_K = K // 2
 SCALE = math.sqrt(float(ROWS * NP))
@@ -63,106 +64,128 @@
     return pl.ds(pl.multiple_of(start, size), size)
 
 
-def sum_and_gather(here, compute, consume, part, held, own, relay, across, zpart, zgot, full, sems, enter=None):
-    done = []
-
-    def chunk(i):
-        return rows((here.z + FAR_FIRST[i]) % NZ * CHUNK, CHUNK)
-
-    part[0] = compute(here.block(2)).astype(BF16)
+def sum_and_gather(here, compute, consume, part, held, own, relay, across, side, zpart, zgot, full, sems, enter=None):
+    def chunk(d):
+        return rows((here.z + d) % NZ * CHUNK, CHUNK)
+
+    sides, relays, plus, minus, zs = {}, {}, {}, {}, {}
+
+    def block(b, d):
+        held[b] = compute(here.block(d))
+        part[b] = held[b].astype(BF16)
+
+    def send_sides(b):
+        for k, d in enumerate((1, NZ - 1)):
+            sides[b, k] = send(part.at[b, chunk(d)], side.at[b, k], sems, 8 * NZ + 2 * b + k, here.at_z(d))
+
+    def send_plus(i, d):
+        plus[i] = send(part.at[1, chunk(d)], across.at[0, i], sems, NZ + i, here.at_x(1))
+
+    def send_minus(i, d):
+        minus[i] = send(part.at[2, chunk(d)], across.at[1, i], sems, 2 * NZ + i, here.at_x(3))
+
+    def send_z(d, value):
+        zpart[d - 1] = value.astype(BF16)
+        zs[d] = send(zpart.at[d - 1], zgot.at[d - 1], sems, 3 * NZ + d, here.at_z(d))
+
+    def arrived(i, d):
+        plus[i].wait_recv()
+        minus[i].wait_recv()
+        value = own[chunk(d), :] + across[0, i].astype(F32) + across[1, i].astype(F32)
+        if i not in RELAYED:
+            relays[i].wait_recv()
+            value = value + across[2, i].astype(F32)
+        return value
+
+    block(0, 2)
     if enter is not None:
         enter()
-    relays = []
-    for i in range(NZ):
+    for i, d in enumerate(FAR):
         if i in RELAYED:
-            relays.append(send(part.at[0, chunk(i)], relay.at[i], sems, i, here.at_x(1 if i % 2 == 0 else 3)))
+            relays[i] = send(part.at[0, chunk(d)], relay.at[i], sems, i, here.at_x(1 if i % 2 == 0 else 3))
         else:
-            relays.append(send(part.at[0, chunk(i)], across.at[2, i], sems, i, here.at_x(2)))
-    held[0] = compute(here.block(1))
-    part[1] = held[0].astype(BF16)
-    held[1] = compute(here.block(3))
-    part[2] = held[1].astype(BF16)
+            relays[i] = send(part.at[0, chunk(d)], across.at[2, i], sems, i, here.at_x(2))
+    send_sides(0)
+    block(1, 1)
+    send_sides(1)
+    block(2, 3)
+    send_sides(2)
     own[...] = compute(here.block(0))
-    plus, minus = {}, {}
-    for i in range(NZ):
+    for i, d in enumerate(FAR):
         if i % 2 == 1 or i not in RELAYED:
-            plus[i] = send(part.at[1, chunk(i)], across.at[0, i], sems, NZ + i, here.at_x(1))
+            send_plus(i, d)
         if i % 2 == 0 or i not in RELAYED:
-            minus[i] = send(part.at[2, chunk(i)], across.at[1, i], sems, 2 * NZ + i, here.at_x(3))
-    zs = []
-    mine = None
-    for step in range(NZ + LAG):
-        if step < NZ:
-            i = step
-            if i in RELAYED:
-                relays[i].wait_recv()
-            if i in RELAYED and i % 2 == 0:
-                part[1, chunk(i)] = (held[0, chunk(i)] + relay[i].astype(F32)).astype(BF16)
-                plus[i] = send(part.at[1, chunk(i)], across.at[0, i], sems, NZ + i, here.at_x(1))
-            elif i in RELAYED:
-                part[2, chunk(i)] = (held[1, chunk(i)] + relay[i].astype(F32)).astype(BF16)
-                minus[i] = send(part.at[2, chunk(i)], across.at[1, i], sems, 2 * NZ + i, here.at_x(3))
+            send_minus(i, d)
+    for d in (1, NZ - 1):
+        send_z(d, own[chunk(d), :])
+    last = len(FAR)
+    for step in range(last + LAG):
+        if step < last and step in RELAYED:
+            d = FAR[step]
+            relays[step].wait_recv()
+            b = 1 if step % 2 == 0 else 2
+            part[b, chunk(d)] = (held[b, chunk(d)] + relay[step].astype(F32)).astype(BF16)
+            (send_plus if b == 1 else send_minus)(step, d)
+        if step == HOME:
+            for b in range(3):
+                value = held[b, chunk(0)]
+                for k in range(2):
+                    sides[b, k].wait_recv()
+                    value = value + side[b, k].astype(F32)
+                part[b, chunk(0)] = value.astype(BF16)
+                if b == 0:
+                    relays[last] = send(part.at[0, chunk(0)], across.at[2, last], sems, last, here.at_x(2))
+                else:
+                    (send_plus if b == 1 else send_minus)(last, 0)
         if step >= LAG:
-            i = step - LAG
-            plus[i].wait_recv()
-            minus[i].wait_recv()
-            mine = own[chunk(i), :] + across[0, i].astype(F32) + across[1, i].astype(F32)
-            if i not in RELAYED:
-                relays[i].wait_recv()
-                mine = mine + across[2, i].astype(F32)
-            if i < NZ - 1:
-                zpart[i] = mine.astype(BF16)
-                zs.append(send(zpart.at[i], zgot.at[i], sems, 3 * NZ + i, here.at_z(FAR_FIRST[i])))
-    for i in range(NZ - 1):
-        zs[i].wait_recv()
-        mine = mine + zgot[i].astype(F32)
-    done += relays + list(plus.values()) + list(minus.values()) + zs
+            send_z(FAR[step - LAG], arrived(step - LAG, FAR[step - LAG]))
+    mine = arrived(last, 0)
+    for d in range(1, NZ):
+        zs[d].wait_recv()
+        mine = mine + zgot[d - 1].astype(F32)
+    done = [c for group in (sides, relays, plus, minus, zs) for c in group.values()]
 
     def place(dx, dz):
         return full.at[rows((here.block(dx) * NZ + (here.z + dz) % NZ) * CHUNK, CHUNK)]
 
     spot = place(0, 0)
     spot[...] = mine.astype(BF16)
-    gs = {}
-    for d in NEAR_FIRST[1:]:
+    gs, xs, sides = {}, {}, {}
+
+    def send_x(step, dz):
+        spot = place(0, dz)
+        for d in (2, 1, 3):
+            xs[step, d] = send(spot, spot, sems, (4 + d) * NZ + step, here.at_x(d))
+
+    def send_back(d):
+        xs[0, d].wait_recv()
+        spot = place(NX - d, 0)
+        for k, dz in enumerate((1, NZ - 1)):
+            sides[d, k] = send(spot, spot, sems, 9 * NZ + 2 * d + k, here.at_z(dz))
+
+    for d in BACK:
         gs[d] = send(spot, spot, sems, 4 * NZ + d, here.at_z(d))
-    plus, minus, forward = [], [], {}
-    for step in range(NZ + LAG):
-        if step < NZ:
-            d = NEAR_FIRST[step]
-            if d:
-                gs[NZ - d].wait_recv()
-            spot = place(0, d)
-            plus.append(send(spot, spot, sems, 5 * NZ + step, here.at_x(1)))
-            minus.append(send(spot, spot, sems, 6 * NZ + step, here.at_x(3)))
-            if step not in FORWARDED:
-                forward[step] = send(spot, spot, sems, 7 * NZ + step, here.at_x(2))
-        if step == NZ - 1:
-            consume(here.block(0))
-        if step >= LAG:
-            i = step - LAG
-            d = NEAR_FIRST[i]
-            if i not in FORWARDED:
-                continue
-            if i % 2 == 0:
-                plus[i].wait_recv()
-                spot, to = place(3, d), here.at_x(1)
-            else:
-                minus[i].wait_recv()
-                spot, to = place(1, d), here.at_x(3)
-            forward[i] = send(spot, spot, sems, 7 * NZ + i, to)
-    for i in range(NZ):
-        if i % 2 == 1 or i not in FORWARDED:
-            plus[i].wait_recv()
-    consume(here.block(3))
-    for i in range(NZ):
-        if i % 2 == 0 or i not in FORWARDED:
-            minus[i].wait_recv()
-    consume(here.block(1))
-    for i in range(NZ):
-        forward[i].wait_recv()
-    consume(here.block(2))
-    return done + list(gs.values()) + plus + minus + list(forward.values())
+    send_x(0, 0)
+    for d in (1, NZ - 1):
+        gs[d] = send(spot, spot, sems, 4 * NZ + d, here.at_z(d))
+    for step, d in enumerate(BACK):
+        gs[NZ - d].wait_recv()
+        send_x(step + 1, d)
+        if step == SIDE:
+            send_back(1)
+            send_back(3)
+        if step == SIDE + 1:
+            send_back(2)
+    for d in (1, NZ - 1):
+        gs[d].wait_recv()
+    consume(here.block(0))
+    for d in (1, 3, 2):
+        for step in range(1, len(BACK) + 1):
+            xs[step, d].wait_recv()
+        for k in range(2):
+            sides[d, k].wait_recv()
+        consume(here.block(NX - d))
+    return done + [c for group in (gs, xs, sides) for c in group.values()]
 
 
 def inverse_factor(gram):
@@ -202,7 +225,7 @@
 
 def whole_kernel(
     stack, omega, basis_out, projected_out,
-    m, om, test, part, held, own, relay, across, zpart, zgot, full,
+    m, om, test, part, held, own, relay, across, side, zpart, zgot, full,
     bt, bparts, bgot, back, total, mine_gram, half_got, halves, gram, factor, pparts, pgot, pall,
     load_sems, sems, pix_sems, gram_sems,
 ):
@@ -235,7 +258,7 @@
     bt[...] = jnp.zeros_like(bt)
     copies = sum_and_gather(
         here, first_block, take_first, part.at[0], held, own, relay.at[0],
-        across.at[0], zpart.at[0], zgot.at[0], full.at[0], sems.at[0],
+        across.at[0], side.at[0], zpart.at[0], zgot.at[0], full.at[0], sems.at[0],
         lambda: pl.semaphore_wait(barrier, len(partners)),
     )
 
@@ -268,7 +291,7 @@
     bt[...] = jnp.zeros_like(bt)
     copies += sum_and_gather(
         here, sketch_block, take_sketch, part.at[1], held, own, relay.at[1],
-        across.at[1], zpart.at[1], zgot.at[1], full.at[1], sems.at[1],
+        across.at[1], side.at[1], zpart.at[1], zgot.at[1], full.at[1], sems.at[1],
     )
 
     y, core = here.pix // 2, here.pix % 2
@@ -340,10 +363,11 @@
             pltpu.VMEM((COLS, K), jnp.int32),
             pltpu.VMEM((COLS, K), BF16),
             pltpu.VMEM((2, 3, BLOCK, K), BF16),
-            pltpu.VMEM((2, BLOCK, K), F32),
+            pltpu.VMEM((3, BLOCK, K), F32),
             pltpu.VMEM((BLOCK, K), F32),
             pltpu.VMEM((2, NZ, CHUNK, K), BF16),
             pltpu.VMEM((2, 3, NZ, CHUNK, K), BF16),
+            pltpu.VMEM((2, 3, 2, CHUNK, K), BF16),
             pltpu.VMEM((2, NZ - 1, CHUNK, K), BF16),
             pltpu.VMEM((2, NZ - 1, CHUNK, K), BF16),
             pltpu.VMEM((2, ROWS, K), BF16),
@@ -361,7 +385,7 @@
             pltpu.VMEM((NP - 1, K, K), BF16),
             pltpu.VMEM((NP, K, K), BF16),
             pltpu.SemaphoreType.DMA((5,)),
-            pltpu.SemaphoreType.DMA((2, 2, 8 * NZ)),
+            pltpu.SemaphoreType.DMA((2, 2, 10 * NZ)),
             pltpu.SemaphoreType.DMA((4, 2, NP - 1)),
             pltpu.SemaphoreType.DMA((2, 5)),
         ],

time: 105 us -> 99.6 us (0.949)
  Pallas kernels: 102 us -> 95.8 us
    pallas_call x1, Pallas kernels: 102 us -> 95.8 us  [body(): pl.pallas_call(whole_kernel, out_shape=(jax.ShapeDtypeStruct((ROWS, K), F...]
where the time goes in v4:
time: 99.6 us; the launch traced here: 99.5 us
  Pallas kernels  95.8 us (96%)
  local copies, waits for them, and re-layouts  2.99 us (3%)
    pallas_call x1, Pallas kernels, body(): pl.pallas_call(whole_kernel, out_shape=(jax.ShapeDtypeStruct((ROWS, K), F...  95.8 us
    unnamed x4, local copies, waits for them, and re-layouts  2.99 us

profile of v4, /device:TPU:1, one launch (start us, length us, event | category | flops | bytes accessed | tf_op | source)
XLA Modules:
  0.0 99.5 jit_solution(5504251786424472985)
XLA Ops:
  0.6 0.0 copy-start
  0.6 1.0 %copy-done = s32[1024,128]{1,0:T(8,128)S(1)} copy-done((s32[1024,128]{1,0:T(8,128)S(1)}, s32[1024,128]{1,0:T(8,128)}, u32[]{:S(2)}) %copy-start) | copy-done | bytes 524312
  1.7 95.8 %shard_map.41 = (f32[4096,128]{1,0:T(8,128)S(1)}, f32[16,1024]{1,0:T(8,128)S(1)}) custom-call(bf16[2048,2,1024]{2,1,0:T(2,128)(2,1)} %stack.1, s32[1024,128]{1,0:T(8,128)S(1)} %copy-done), custom_call_target="tpu_custom_call" | custom-call | flops 4294967296 | bytes 12582912 | tf_op jit(solution)/shard_map/pallas_call | solution.py:353
  97.5 1.3 %copy.6 = f32[2048,2,128]{2,1,0:T(2,128)} copy(f32[2048,2,128]{2,1,0:T(2,128)S(1)} %bitcast.1) | data formatting | bytes 4194304
  98.8 0.6 copy.7
Async XLA Ops:
  0.6 1.0 %copy-start = (s32[1024,128]{1,0:T(8,128)S(1)}, s32[1024,128]{1,0:T(8,128)}, u32[]{:S(2)}) copy-start(s32[1024,128]{1,0:T(8,128)} %omega.1) | copy-start | bytes 1572868

commit v5 on v4

--- a/solution.py
+++ b/solution.py
@@ -22,6 +22,7 @@
 LAG = 2
 HOME = 1
 SIDE = 1
+PIX_ORDER = (4, 3, 5, 2, 6, 1, 7)
 PANEL = 32
 HALF_K = K // 2
 SCALE = math.sqrt(float(ROWS * NP))
@@ -265,19 +266,19 @@
     for j in range(NP):
         bparts[j] = bt[:, j * K:(j + 1) * K].astype(BF16)
         total[j] = bt[:, j * K:(j + 1) * K]
-    bs = []
-    for d in range(1, NP):
-        bs.append(send(bparts.at[(here.pix + d) % NP], bgot.at[d - 1], pix_sems.at[0], d - 1, here.at_pix(d)))
+    bs = {}
+    for d in PIX_ORDER:
+        bs[d] = send(bparts.at[(here.pix + d) % NP], bgot.at[d - 1], pix_sems.at[0], d - 1, here.at_pix(d))
     mine = total[here.pix]
     for d in range(1, NP):
-        bs[d - 1].wait_recv()
+        bs[d].wait_recv()
         mine = mine + bgot[d - 1].astype(F32)
     spot = back.at[rows(here.pix * K, K)]
     spot[...] = mine.T.astype(BF16)
-    gs = [send(spot, spot, pix_sems.at[1], d - 1, here.at_pix(d)) for d in range(1, NP)]
+    gs = [send(spot, spot, pix_sems.at[1], d - 1, here.at_pix(d)) for d in PIX_ORDER]
     for c in gs:
         c.wait_recv()
-    copies += bs + gs
+    copies += list(bs.values()) + gs
 
     def sketch_block(b):
         return jnp.dot(m[rows(b * BLOCK, BLOCK), :], back[...], preferred_element_type=F32)
@@ -306,9 +307,9 @@
     for j in range(NP):
         pparts[j] = bt[:, j * K:(j + 1) * K].astype(BF16)
         total[j] = bt[:, j * K:(j + 1) * K]
-    ps = []
-    for d in range(1, NP):
-        ps.append(send(pparts.at[(here.pix + d) % NP], pgot.at[d - 1], pix_sems.at[2], d - 1, here.at_pix(d)))
+    ps = {}
+    for d in PIX_ORDER:
+        ps[d] = send(pparts.at[(here.pix + d) % NP], pgot.at[d - 1], pix_sems.at[2], d - 1, here.at_pix(d))
     for c in ys:
         c.wait_recv()
     gram[keep, :] = (halves[0] + halves[1]) + (halves[2] + halves[3])
@@ -316,13 +317,13 @@
     swap_back = send(spot, spot, gram_sems, 4, near)
     mine = total[here.pix]
     for d in range(1, NP):
-        ps[d - 1].wait_recv()
+        ps[d].wait_recv()
         mine = mine + pgot[d - 1].astype(F32)
     pall[here.pix] = mine.astype(BF16)
     spot = pall.at[here.pix]
-    gs = [send(spot, spot, pix_sems.at[3], d - 1, here.at_pix(d)) for d in range(1, NP)]
+    gs = [send(spot, spot, pix_sems.at[3], d - 1, here.at_pix(d)) for d in PIX_ORDER]
     swap_back.wait_recv()
-    copies += [swap, swap_back] + ys + ps + gs
+    copies += [swap, swap_back] + ys + list(ps.values()) + gs
     inverse = inverse_factor(gram[...])
     factor[...] = inverse
 

time: 99.6 us -> 98.4 us (0.988)
  Pallas kernels: 95.8 us -> 94.6 us
    pallas_call x1, Pallas kernels: 95.8 us -> 94.6 us  [body(): pl.pallas_call(whole_kernel, out_shape=(jax.ShapeDtypeStruct((ROWS, K), F...]
where the time goes in v5:
time: 98.4 us; the launch traced here: 98.3 us
  Pallas kernels  94.6 us (96%)
  local copies, waits for them, and re-layouts  2.99 us (3%)
    pallas_call x1, Pallas kernels, body(): pl.pallas_call(whole_kernel, out_shape=(jax.ShapeDtypeStruct((ROWS, K), F...  94.6 us
    unnamed x4, local copies, waits for them, and re-layouts  2.99 us

profile of v5, /device:TPU:1, one launch (start us, length us, event | category | flops | bytes accessed | tf_op | source)
XLA Modules:
  0.0 98.3 jit_solution(5484871544664108665)
XLA Ops:
  0.6 0.0 copy-start
  0.6 1.0 %copy-done = s32[1024,128]{1,0:T(8,128)S(1)} copy-done((s32[1024,128]{1,0:T(8,128)S(1)}, s32[1024,128]{1,0:T(8,128)}, u32[]{:S(2)}) %copy-start) | copy-done | bytes 524312
  1.7 94.6 %shard_map.41 = (f32[4096,128]{1,0:T(8,128)S(1)}, f32[16,1024]{1,0:T(8,128)S(1)}) custom-call(bf16[2048,2,1024]{2,1,0:T(2,128)(2,1)} %stack.1, s32[1024,128]{1,0:T(8,128)S(1)} %copy-done), custom_call_target="tpu_custom_call" | custom-call | flops 4294967296 | bytes 12582912 | tf_op jit(solution)/shard_map/pallas_call | solution.py:354
  96.3 1.3 %copy.6 = f32[2048,2,128]{2,1,0:T(2,128)} copy(f32[2048,2,128]{2,1,0:T(2,128)S(1)} %bitcast.1) | data formatting | bytes 4194304
  97.6 0.6 copy.7
Async XLA Ops:
  0.6 1.0 %copy-start = (s32[1024,128]{1,0:T(8,128)S(1)}, s32[1024,128]{1,0:T(8,128)}, u32[]{:S(2)}) copy-start(s32[1024,128]{1,0:T(8,128)} %omega.1) | copy-start | bytes 1572868

commit v6 on v5

--- a/solution.py
+++ b/solution.py
@@ -310,6 +310,8 @@
     ps = {}
     for d in PIX_ORDER:
         ps[d] = send(pparts.at[(here.pix + d) % NP], pgot.at[d - 1], pix_sems.at[2], d - 1, here.at_pix(d))
+    for c in copies:
+        c.wait_send()
     for c in ys:
         c.wait_recv()
     gram[keep, :] = (halves[0] + halves[1]) + (halves[2] + halves[3])
@@ -323,7 +325,7 @@
     spot = pall.at[here.pix]
     gs = [send(spot, spot, pix_sems.at[3], d - 1, here.at_pix(d)) for d in PIX_ORDER]
     swap_back.wait_recv()
-    copies += [swap, swap_back] + ys + list(ps.values()) + gs
+    copies = [swap, swap_back] + ys + list(ps.values()) + gs
     inverse = inverse_factor(gram[...])
     factor[...] = inverse
 

time: 98.4 us -> 98.2 us (level)
  no operation moved by 1% of the time
where the time goes in v6:
time: 98.2 us; the launch traced here: 98.1 us
  Pallas kernels  94.4 us (96%)
  local copies, waits for them, and re-layouts  2.99 us (3%)
    pallas_call x1, Pallas kernels, body(): pl.pallas_call(whole_kernel, out_shape=(jax.ShapeDtypeStruct((ROWS, K), F...  94.4 us
    unnamed x4, local copies, waits for them, and re-layouts  2.99 us

profile of v6, /device:TPU:1, one launch (start us, length us, event | category | flops | bytes accessed | tf_op | source)
XLA Modules:
  0.0 98.1 jit_solution(7603037751467304699)
XLA Ops:
  0.6 0.0 copy-start
  0.6 1.0 %copy-done = s32[1024,128]{1,0:T(8,128)S(1)} copy-done((s32[1024,128]{1,0:T(8,128)S(1)}, s32[1024,128]{1,0:T(8,128)}, u32[]{:S(2)}) %copy-start) | copy-done | bytes 524312
  1.7 94.4 %shard_map.41 = (f32[4096,128]{1,0:T(8,128)S(1)}, f32[16,1024]{1,0:T(8,128)S(1)}) custom-call(bf16[2048,2,1024]{2,1,0:T(2,128)(2,1)} %stack.1, s32[1024,128]{1,0:T(8,128)S(1)} %copy-done), custom_call_target="tpu_custom_call" | custom-call | flops 4294967296 | bytes 12582912 | tf_op jit(solution)/shard_map/pallas_call | solution.py:356
  96.1 1.3 %copy.6 = f32[2048,2,128]{2,1,0:T(2,128)} copy(f32[2048,2,128]{2,1,0:T(2,128)S(1)} %bitcast.1) | data formatting | bytes 4194304
  97.4 0.6 copy.7
Async XLA Ops:
  0.6 1.0 %copy-start = (s32[1024,128]{1,0:T(8,128)S(1)}, s32[1024,128]{1,0:T(8,128)}, u32[]{:S(2)}) copy-start(s32[1024,128]{1,0:T(8,128)} %omega.1) | copy-start | bytes 1572868
